TPU v7x, 512 devices: a whole 4x8x8 slice. The times are simulated.
512 devices in a mesh: det: 4 (over y_lo, core), tm: 128 (over z, x, y_hi).
Axes of the slice: x: 4, y: 8 (y_hi: 4, y_lo: 2; y = y_hi * 2 + y_lo), z: 8, core: 2. Of those that a mesh axis runs over, the one named last changes fastest.
Arguments:
- spectra: bfloat16 [4, 256, 32, 2, 128], P('det', 'tm'), may hold values from -200 to 200
- valid: int32 [256], P('tm'), may hold values 0 or 1
- lags: float32 [49152], replicated, may hold values from -0.01 to 0.01
- drift: float32 [49152], replicated, may hold values from -4 to 4
- block_table: int32 [1024, 2], replicated, may hold values from 0 to 95, as said below
Outputs:
- sky_map: float32 [49152], P(('det', 'tm'))
Inputs may be any that keep to these rules, and one draw needn't show every extreme that they name: `block_table`: row (2 i + h) * 4 + k, for 0 <= i < 128, h in 0, 1 and 0 <= k < 4, holds a band from h * 32 to h * 32 + 31 and a tile below 96; each aligned block of 2 rows starting at a multiple of 2 has one band, and the 2 bands of one (i, h) are distinct.
All inputs are finite; a program needn't handle non-finite values. No bound on the sum of `valid` on one device may be relied on, other than what follows from the above.
Results may differ from a plain program's by a relative error of at most 0.0037.
Values may be sent and summed in bfloat16 or wider, within the bound.
A program may use at most 64 MiB of HBM per device.

v0:
```python
import math

import jax
import jax.numpy as jnp
from jax import lax
from jax.sharding import PartitionSpec as P

PT = 512


full_turn = 2.0 * math.pi


def from_partner(x, axis, distance):
    return lax.ppermute(x, axis, [(i, i ^ 1 << distance) for i in range(lax.axis_size(axis))])


def tile_partial(band_slab, band_id, pixel_lags, pixel_drift, time_coord, band_total, band_width):
    frequency = (band_id * band_width + jnp.arange(band_width, dtype=jnp.int32)).astype(jnp.float32)
    angle_grid = full_turn * frequency[:, None] * pixel_lags[None, :]
    cosine_grid = jnp.cos(angle_grid)
    sine_grid = jnp.sin(angle_grid)
    kernel = jnp.concatenate(
        [
            jnp.concatenate([cosine_grid, -sine_grid], 1),
            jnp.concatenate([sine_grid, cosine_grid], 1),
        ],
        0,
    ).astype(jnp.bfloat16)
    product = jnp.dot(band_slab, kernel, preferred_element_type=jnp.float32)
    columns = pixel_lags.shape[0]
    factor = full_turn * (band_id.astype(jnp.float32) + 0.5) / band_total
    rotation = (factor * pixel_drift)[None, :] * time_coord[:, None]
    return jnp.sum(
        jnp.cos(rotation) * product[:, :columns] - jnp.sin(rotation) * product[:, columns:], axis=0
    )


def shards(spectra, valid, lags, drift, block_table):
    det_index = lax.axis_index("det")
    bin_half = det_index % 2
    detector_bit = det_index // 2
    tm_count = lax.axis_size("tm")
    tm_index = lax.axis_index("tm")
    own_spectra = spectra[0]
    seg_count = own_spectra.shape[0]
    bands_half = own_spectra.shape[1]
    band_width = own_spectra.shape[3]
    seg_kept = seg_count // 2
    segment_total = seg_count * tm_count
    band_total = 2 * bands_half
    squares = jnp.sum(jnp.square(own_spectra.astype(jnp.float32)), axis=(1, 2, 3))
    stacked = jnp.stack(
        [jnp.where(detector_bit == 0, squares, 0.0), jnp.where(detector_bit == 1, squares, 0.0)]
    )
    powers = lax.psum(stacked, "det") / (band_total * band_width) + 1e-06
    seg_start = detector_bit * seg_kept
    kept_rows = lax.dynamic_slice_in_dim(own_spectra, seg_start, seg_kept, 0)
    sent_rows = lax.dynamic_slice_in_dim(own_spectra, seg_kept - seg_start, seg_kept, 0)
    arrived = from_partner(sent_rows, "det", 1)
    hanford = jnp.where(detector_bit == 0, kept_rows, arrived).astype(jnp.float32)
    livingston = jnp.where(detector_bit == 0, arrived, kept_rows).astype(jnp.float32)
    kept_powers = lax.dynamic_slice_in_dim(powers, seg_start, seg_kept, 1)
    valid_rows = lax.dynamic_slice_in_dim(valid, seg_start, seg_kept, 0).astype(jnp.float32)
    weight = valid_rows / (kept_powers[0] * kept_powers[1])
    cross_real = (
        hanford[:, :, 0] * livingston[:, :, 0] + hanford[:, :, 1] * livingston[:, :, 1]
    ) * weight[:, None, None]
    cross_imag = (
        hanford[:, :, 0] * livingston[:, :, 1] - hanford[:, :, 1] * livingston[:, :, 0]
    ) * weight[:, None, None]
    cross = (
        jnp.stack([cross_real, cross_imag], 2)
        .astype(jnp.bfloat16)
        .reshape(seg_kept, bands_half, 2 * band_width)
    )
    by_band = jnp.transpose(cross, (1, 0, 2))
    blocks_all = block_table.reshape(tm_count, 2, -1, 2)
    chosen = lax.dynamic_index_in_dim(blocks_all, bin_half, 1, keepdims=False)
    own_blocks = lax.dynamic_index_in_dim(chosen, tm_index, 0, keepdims=False)
    block_count = own_blocks.shape[0]
    picked = chosen[:, :, 0] - bin_half * bands_half
    outgoing = jnp.take(by_band, picked.reshape(-1), axis=0).reshape(
        tm_count, block_count, seg_kept, 2 * band_width
    )
    received = lax.all_to_all(outgoing, "tm", split_axis=0, concat_axis=2, tiled=True)
    item_bands = own_blocks[:, 0]
    item_tiles = own_blocks[:, 1].reshape(-1, 1)
    row_ids = jnp.arange(tm_count * seg_kept, dtype=jnp.int32)
    segment_ids = row_ids // seg_kept * seg_count + detector_bit * seg_kept + row_ids % seg_kept
    time_coord = (segment_ids.astype(jnp.float32) + 0.5 - segment_total / 2) / segment_total

    def one_item(item):
        band_slab, band_id, tile_ids = item
        pixels = (tile_ids[:, None] * PT + jnp.arange(PT, dtype=jnp.int32)[None, :]).reshape(-1)
        return tile_partial(
            band_slab,
            band_id,
            jnp.take(lags, pixels),
            jnp.take(drift, pixels),
            time_coord,
            band_total,
            band_width,
        )

    partials = lax.map(one_item, (received[0], item_bands, item_tiles))
    tile_total = lags.shape[0] // PT
    onehot = (own_blocks[:, 1][:, None] == jnp.arange(tile_total, dtype=jnp.int32)[None, :]).astype(
        jnp.float32
    )
    sky_map = jnp.dot(
        onehot.T, partials, precision=lax.Precision.HIGHEST, preferred_element_type=jnp.float32
    ).reshape(-1)
    summed = lax.psum(sky_map, ("det", "tm"))
    per_device = summed.shape[0] // (lax.axis_size("det") * tm_count)
    result = lax.dynamic_slice_in_dim(
        summed, (det_index * tm_count + tm_index) * per_device, per_device
    )
    return result / math.sqrt(segment_total * band_width)


def solution(mesh):
    placed = (P("det", "tm", None, None, None), P("tm"), P(), P(), P())
    return jax.shard_map(
        shards, mesh=mesh, in_specs=placed, out_specs=P(("det", "tm")), check_vma=False
    )
```

profile of v0, /device:TPU:1, one launch (start us, length us, event | category | flops | bytes accessed | tf_op | source)
XLA Modules:
  0.0 379.3 jit_solution(5968269931772476775)
XLA Ops:
  6.5 0.8 copy-done.2
  7.3 4.0 %collective-permute-start = (bf16[1,32,2,128]{3,2,1,0:T(2,128)(2,1)S(1)}, bf16[1,32,2,128]{3,2,1,0:T(2,128)(2,1)S(1)}, u32[]{:S(2)}, u32[]{:S(2)}) collective-permute-start(bf16[1,32,2,128]{3,2,1,0:T(2,128)(2,1)S(1)} %dynamic-slice_bitcast_fusion), channel_id=1, source_target_pairs={{0,256},{128,384},{256,0},{384,128},{1,257},{129,385},{257,1},{385... | collective-permute-start | bytes 49160 | tf_op jit(solution)/shard_map/ppermute | solution.py:15
  12.8 10.2 %psum.14 = f32[2,2]{1,0:T(2,128)S(1)} all-reduce(f32[2,2]{1,0:T(2,128)S(1)} %pad_maximum_fusion.1), channel_id=1, replica_groups=mesh['det'=4,'tm'=128] {'det'}, use_global_device_ids=true, to_apply=%region_1.2 | all-reduce | flops 4 | bytes 32 | tf_op jit(solution)/shard_map/psum | solution.py:56
  27.1 2.0 gather_fusion.2
  29.1 0.9 bitcast_select_fusion
  30.1 14.9 %all-to-all-start = ((bf16[128,4,1,256]{3,1,2,0:T(4,128)(2,1)}), bf16[128,4,1,256]{3,1,2,0:T(4,128)(2,1)S(1)}, u32[]{:S(2)}, u32[]{:S(2)}) async-start(bf16[128,4,1,256]{3,1,2,0:T(4,128)(2,1)} %bitcast_select_fusion), calls=%async_computation | async-start | bytes 524288 | tf_op jit(solution)/shard_map/all_to_all | solution.py:86
  45.1 14.8 %all-to-all-done = bf16[128,4,1,256]{3,1,2,0:T(4,128)(2,1)S(1)} async-done(((bf16[128,4,1,256]{3,1,2,0:T(4,128)(2,1)}), bf16[128,4,1,256]{3,1,2,0:T(4,128)(2,1)S(1)}, u32[]{:S(2)}, u32[]{:S(2)}) %all-to-all-start) | async-done | bytes 262176 | tf_op jit(solution)/shard_map/all_to_all | solution.py:86
  59.9 0.9 copy-done
  60.9 51.5 %while.13 = (s32[]{:T(128)}, f32[4,512]{1,0:T(4,128)S(1)}, s32[4]{0:T(128)S(1)}, s32[4,1]{0,1:T(1,128)S(1)}, f32[49152]{0:T(1024)S(1)}, /*index=5*/bf16[4,128,25...) while((s32[]{:T(128)}, f32[4,512]{1,0:T(4,128)S(1)}, ...), condition=%wide.region_4.6_spmd.clone, body=%wide.region_2.5_spmd.clone.sunk | while | flops 69870088 | bytes 1941725 | solution.py:106
  62.1 3.1 gather_fusion
  65.3 3.1 gather_fusion.1
  68.4 0.7 dynamic_slice.75
  71.1 1.1 fusion.39
  72.5 1.2 fusion.41
  75.0 3.1 gather_fusion
  78.2 3.1 gather_fusion.1
  81.3 0.7 dynamic_slice.75
  84.0 1.1 fusion.39
  85.4 1.2 fusion.41
  87.9 3.1 gather_fusion
  91.1 3.1 gather_fusion.1
  94.2 0.7 dynamic_slice.75
  96.9 1.1 fusion.39
  98.3 1.2 fusion.41
  100.8 3.1 gather_fusion
  104.0 3.1 gather_fusion.1
  107.1 0.7 dynamic_slice.75
  109.8 1.1 fusion.39
  111.2 1.2 fusion.41
  112.8 0.7 copy.14
  113.5 257.7 %all-reduce.2.cloned.1.call-done = f32[49152]{0:T(1024)} async-done(((f32[49152]{0:T(1024)}), f32[49152]{0:T(1024)}) %all-reduce.2.cloned.1.call-update) | async-done | bytes 196624 | tf_op jit(solution)/shard_map/psum | solution.py:114
  371.2 1.3 dynamic-slice_multiply_fusion
  (67 shorter events, 12.9 us)
Async XLA Ops:
  6.5 0.8 copy-start.2
  7.3 19.6 %collective-permute-start = (bf16[1,32,2,128]{3,2,1,0:T(2,128)(2,1)S(1)}, bf16[1,32,2,128]{3,2,1,0:T(2,128)(2,1)S(1)}, u32[]{:S(2)}, u32[]{:S(2)}) collective-permute-start(bf16[1,32,2,128]{3,2,1,0:T(2,128)(2,1)S(1)} %dynamic-slice_bitcast_fusion), channel_id=1, source_target_pairs={{0,256},{128,384},{256,0},{384,128},{1,257},{129,385},{257,1},{385... | collective-permute-start | bytes 49160 | tf_op jit(solution)/shard_map/ppermute | solution.py:15
  11.4 0.7 copy-start.3
  23.7 0.7 copy-start.4
  30.1 29.8 %all-to-all-start = ((bf16[128,4,1,256]{3,1,2,0:T(4,128)(2,1)}), bf16[128,4,1,256]{3,1,2,0:T(4,128)(2,1)S(1)}, u32[]{:S(2)}, u32[]{:S(2)}) async-start(bf16[128,4,1,256]{3,1,2,0:T(4,128)(2,1)} %bitcast_select_fusion), calls=%async_computation | async-start | bytes 524288 | tf_op jit(solution)/shard_map/all_to_all | solution.py:86
  45.0 326.2 %all-reduce.2.cloned.1.call-start = ((), (), s32[]{:S(2)}) async-start(), calls=%async_computation.1 | async-start | bytes 393216 | tf_op jit(solution)/shard_map/psum | solution.py:114
  59.8 0.9 copy-start
  59.8 1.0 copy-start.1
Sparse Core Ops, SparseCore 0:
  113.6 257.5 all-reduce.1
where the time goes:
time: 380 us; the launch traced here: 379 us
  waiting for transfers between devices  272 us (72%)
  local copies, waits for them, and re-layouts  35.6 us (9%)
  other arithmetic  19.4 us (5%)
  starting transfers between devices  19 us (5%)
  between operations  15.6 us (4%)
  blocking collectives  10.2 us (3%)
  loops' own time  5.79 us (2%)
    psum x1, waiting for transfers between devices, shards(): summed = lax.psum(sky_map, ('det', 'tm'))  258 us
    all_to_all x1, starting transfers between devices, shards(): lax.all_to_all(outgoing, 'tm', split_axis=0, concat_axis=2, tiled=True)  14.9 us
    all_to_all x1, waiting for transfers between devices, shards(): lax.all_to_all(outgoing, 'tm', split_axis=0, concat_axis=2, tiled=True)  14.8 us
    gather x4, local copies, waits for them, and re-layouts, one_item(): jnp.take(lags, pixels)  12.6 us
    gather x4, local copies, waits for them, and re-layouts, one_item(): jnp.take(drift, pixels)  12.6 us
    psum x1, blocking collectives, shards(): powers = lax.psum(stacked, 'det') / (band_total * band_width) + 1e-06  10.2 us
  transfers between devices with their start and end apart: 3, of which 2 were waited for; matrix products, arithmetic and copies ran while one was open for 1% of the time, Pallas kernels for 0%

commit v1 on v0

v1 whole, which is shorter than its diff:
```python
import math

import jax
import jax.numpy as jnp
from jax import lax
from jax.experimental import pallas as pl
from jax.experimental.pallas import tpu as pltpu
from jax.sharding import PartitionSpec as P

MESH = pl.DeviceIdType.MESH

N_DET = 4
N_TM = 128
N_Z = 8
N_XY = 16
N_ZD = N_Z * N_DET
BINS = 128
BANDS = 32
TILES_OWN = 3
PIX_OWN = 96
CHUNKS = 8

SIN = [(-1.0) ** n * (2 * math.pi) ** (2 * n + 1) / math.factorial(2 * n + 1) for n in range(6)]
COS = [(-1.0) ** n * (2 * math.pi) ** (2 * n) / math.factorial(2 * n) for n in range(7)]


def horner(coefficients, x):
    total = jnp.full_like(x, coefficients[-1])
    for c in coefficients[-2::-1]:
        total = total * x + c
    return total


def cos_sin(turns):
    half = jnp.floor(turns * 2.0 + 0.5)
    r = turns - half * 0.5
    sign = 1.0 - 2.0 * (half - 2.0 * jnp.floor(half * 0.5))
    square = r * r
    return sign * horner(COS, square), sign * r * horner(SIN, square)


def iota(shape, dim):
    return lax.broadcasted_iota(jnp.int32, shape, dim)


def kernel(
    spec_hbm, valid_hbm, lags_hbm, drift_hbm, table_hbm, out_ref,
    own_v, other_v, lags_v, drift_v, table_v, table_s, valid_s,
    squares, squares_all, send1, recv1, send2, recv2,
    kmat, rot_cos, rot_sin, masks, part, parts, folded, send4, recv4,
    local_sem, hl_send, hl_recv, sq_send, sq_recv, s1_send, s1_recv,
    s2_send, s2_recv, s3_send, s3_recv, s4_send, s4_recv,
):
    det = lax.axis_index("det")
    tm = lax.axis_index("tm")
    k, h = det // 2, det % 2
    z, xy = tm // N_XY, tm % N_XY
    zd = z * N_DET + det

    def zd_peer(r):
        p = (zd + r) % N_ZD
        return (p % N_DET, p // N_DET * N_XY + xy)

    def xy_peer(r):
        return (det, z * N_XY + (xy + r) % N_XY)

    barrier = pltpu.get_barrier_semaphore()

    @pl.loop(1, N_ZD)
    def _(r):
        pl.semaphore_signal(barrier, inc=1, device_id=zd_peer(r), device_id_type=MESH)

    @pl.loop(1, N_XY)
    def _(r):
        pl.semaphore_signal(barrier, inc=1, device_id=xy_peer(r), device_id_type=MESH)

    loads = [
        pltpu.make_async_copy(src, dst, local_sem.at[n])
        for n, (src, dst) in enumerate(
            [
                (spec_hbm, own_v), (table_hbm, table_s), (table_hbm, table_v),
                (valid_hbm, valid_s), (lags_hbm, lags_v), (drift_hbm, drift_v),
            ]
        )
    ]
    for load in loads:
        load.start()
    loads[0].wait()

    own = own_v[...].astype(jnp.float32)
    sq = own * own
    row8 = iota((8, BINS), 0)
    seg0 = jnp.sum(sq[:64], axis=0, keepdims=True)
    seg1 = jnp.sum(sq[64:], axis=0, keepdims=True)
    sums = jnp.where(row8 == 0, seg0, jnp.where(row8 == 1, seg1, 0.0))
    squares[...] = sums
    squares_all[det] = sums

    pl.semaphore_wait(barrier, N_ZD - 1 + N_XY - 1)

    hl = pltpu.make_async_remote_copy(
        src_ref=own_v, dst_ref=other_v, send_sem=hl_send, recv_sem=hl_recv,
        device_id=((det + 2) % N_DET, tm), device_id_type=MESH,
    )
    hl.start()
    sq_copies = [
        pltpu.make_async_remote_copy(
            src_ref=squares, dst_ref=squares_all.at[det],
            send_sem=sq_send.at[r - 1], recv_sem=sq_recv.at[r - 1],
            device_id=((det + r) % N_DET, tm), device_id_type=MESH,
        )
        for r in range(1, N_DET)
    ]
    for copy in sq_copies:
        copy.start()
    for load in loads[1:]:
        load.wait()

    lane = iota((N_XY, BINS), 1)
    wanted = lane == 8 * iota((N_XY, BINS), 0) + 4 * h + 2 * k
    picks = []
    for dz in range(N_Z):
        bands = table_v[2 * dz : 2 * dz + 1, :].astype(jnp.float32)
        column = jnp.sum(jnp.where(wanted, bands, 0.0), axis=1, keepdims=True)
        picks.append((column - (BANDS * h).astype(jnp.float32)) * 2.0)
    pick = jnp.concatenate(picks, axis=0)
    source = iota((N_TM, BINS), 1).astype(jnp.float32)
    pick0 = jnp.where(source == pick, 1.0, 0.0).astype(jnp.bfloat16)
    pick1 = jnp.where(source == pick + 64.0, 1.0, 0.0).astype(jnp.bfloat16)

    hl.wait_recv()
    other = other_v[...].astype(jnp.float32)
    own_up = pltpu.roll(own, BINS - 1, 0)
    other_up = pltpu.roll(other, BINS - 1, 0)
    sign = (1 - 2 * k).astype(jnp.float32)
    cross_real = own * other + own_up * other_up
    cross_imag = (own * other_up - own_up * other) * sign
    for copy in sq_copies:
        copy.wait_recv()
    total = lambda a: jnp.sum(a, axis=1, keepdims=True) / 8192.0 + 1e-06
    power_h = total(squares_all[0] + squares_all[1])
    power_l = total(squares_all[2] + squares_all[3])
    flags = jnp.where(iota((8, 1), 0) == 0, valid_s[0], valid_s[1]).astype(jnp.float32)
    weight = flags / (power_h * power_l)
    weights = jnp.where(iota((BINS, 1), 0) < 64, weight[0:1], weight[1:2])
    cross = jnp.concatenate([cross_real * weights, cross_imag * weights], axis=1)
    cross = cross.astype(jnp.bfloat16)
    for s, p in enumerate((pick0, pick1)):
        rows = jnp.dot(p, cross, preferred_element_type=jnp.float32)
        rows = rows.astype(jnp.bfloat16).reshape(N_Z, N_XY, 2 * BINS)
        send1[:, :, 2 * BINS * s : 2 * BINS * (s + 1)] = rows

    def stage1(r):
        return pltpu.make_async_remote_copy(
            src_ref=send1.at[(z + r) % N_Z], dst_ref=recv1.at[z],
            send_sem=s1_send, recv_sem=s1_recv,
            device_id=(det, (z + r) % N_Z * N_XY + xy), device_id_type=MESH,
        )

    @pl.loop(1, N_Z)
    def _(r):
        stage1(r).start()

    recv1[z] = send1[z]

    g = table_s[2 * z, 8 * xy + 4 * h + 2 * k]
    g_f = g.astype(jnp.float32)
    first = [table_s[2 * z + 1, 8 * xy + 4 * h + 2 * k + n] for n in range(2)]
    col16 = iota((16, BINS), 0)
    col8 = iota((8, BINS), 0)

    @pl.loop(0, CHUNKS)
    def _(ch):
        tile = jnp.where(ch < 4, first[0], first[1])
        lag = lags_v[pl.ds(4 * tile + ch % 4, 1), :]
        ca, sa = cos_sin((g * BINS + 16 * col8).astype(jnp.float32) * lag)
        cb, sb = cos_sin(col16.astype(jnp.float32) * lag)
        for a in range(8):
            c1, s1 = ca[a : a + 1], sa[a : a + 1]
            cosine = (c1 * cb - s1 * sb).astype(jnp.bfloat16)
            sine = (s1 * cb + c1 * sb).astype(jnp.bfloat16)
            kmat[ch, 16 * a : 16 * a + 16, 0:BINS] = cosine
            kmat[ch, 16 * a : 16 * a + 16, BINS:] = -sine
            kmat[ch, BINS + 16 * a : BINS + 16 * a + 16, 0:BINS] = sine
            kmat[ch, BINS + 16 * a : BINS + 16 * a + 16, BINS:] = cosine

    pltpu.make_async_copy(
        recv1.at[pl.ds(0, N_Z - 1)], recv1.at[pl.ds(0, N_Z - 1)], s1_recv
    ).wait()

    o, n = iota((256, 256), 0), iota((256, 256), 1)
    perm = jnp.where(n == (o % 16 // 8) * 128 + (o % 8) * 16 + o // 16, 1.0, 0.0)
    perm = perm.astype(jnp.bfloat16)
    got = recv1[...].reshape(N_TM, 4 * BINS)
    got = jnp.concatenate([got[:, : 2 * BINS], got[:, 2 * BINS :]], axis=0)
    rows = jnp.dot(perm, got, preferred_element_type=jnp.float32).astype(jnp.bfloat16)
    send2[...] = rows.reshape(N_XY, 16, 2 * BINS)

    def stage2(r):
        return pltpu.make_async_remote_copy(
            src_ref=send2.at[(xy + r) % N_XY], dst_ref=recv2.at[xy],
            send_sem=s2_send, recv_sem=s2_recv,
            device_id=xy_peer(r), device_id_type=MESH,
        )

    @pl.loop(1, N_XY)
    def _(r):
        stage2(r).start()

    recv2[xy] = send2[xy]

    time_a = (32 * (col16 % 8) + col16 // 8).astype(jnp.float32) - 127.5
    time_b = (2 * col16).astype(jnp.float32)
    scale = (g_f + 0.5) * (1.0 / (64 * 256))

    @pl.loop(0, CHUNKS)
    def _(ch):
        tile = jnp.where(ch < 4, first[0], first[1])
        rate = drift_v[pl.ds(4 * tile + ch % 4, 1), :] * scale
        ca, sa = cos_sin(time_a * rate)
        cb, sb = cos_sin(time_b * rate)
        for a in range(16):
            c1, s1 = cb[a : a + 1], sb[a : a + 1]
            rot_cos[ch, 16 * a : 16 * a + 16, :] = c1 * ca - s1 * sa
            rot_sin[ch, 16 * a : 16 * a + 16, :] = s1 * ca + c1 * sa

    tile_mine = 24 * det + TILES_OWN * z

    @pl.loop(0, N_ZD)
    def _(p):
        at = 8 * xy + 4 * (p % 2) + p % 4 // 2 * 2
        t0 = table_s[2 * (p // 4) + 1, at]
        t1 = table_s[2 * (p // 4) + 1, at + 1]
        tiles = jnp.where(row8 < 4, t0, t1)
        for j in range(TILES_OWN):
            masks[p, j] = jnp.where(tiles == tile_mine + j, 1.0, 0.0)

    pltpu.make_async_copy(
        recv2.at[pl.ds(0, N_XY - 1)], recv2.at[pl.ds(0, N_XY - 1)], s2_recv
    ).wait()

    slab = recv2[...].reshape(256, 2 * BINS)

    for ch in range(CHUNKS):
        product = jnp.dot(slab, kmat[ch], preferred_element_type=jnp.float32)
        turned = rot_cos[ch] * product[:, :BINS] - rot_sin[ch] * product[:, BINS:]
        part[ch : ch + 1, :] = jnp.sum(turned, axis=0, keepdims=True)

    def stage3(r):
        return pltpu.make_async_remote_copy(
            src_ref=part, dst_ref=parts.at[zd],
            send_sem=s3_send, recv_sem=s3_recv,
            device_id=zd_peer(r), device_id_type=MESH,
        )

    @pl.loop(1, N_ZD)
    def _(r):
        stage3(r).start()

    parts[zd] = part[...]
    pltpu.make_async_copy(
        parts.at[pl.ds(0, N_ZD - 1)], parts.at[pl.ds(0, N_ZD - 1)], s3_recv
    ).wait()

    sums = [jnp.zeros((8, BINS), jnp.float32) for _ in range(TILES_OWN)]
    for p in range(N_ZD):
        terms = parts[p]
        for j in range(TILES_OWN):
            sums[j] += terms * masks[p, j]
    for j in range(TILES_OWN):
        folded[4 * j : 4 * j + 4, :] = sums[j][0:4] + sums[j][4:8]
    rows = [folded[pl.ds(i, 4, stride=3), :] for i in range(3)]
    lane4 = iota((4, BINS), 1)
    for y in range(4):
        at, shift = 96 * y // BINS, 96 * y % BINS
        low = pltpu.roll(rows[at], BINS - shift, 1) if shift else rows[at]
        if BINS - shift < PIX_OWN:
            high = pltpu.roll(rows[at + 1], BINS - shift, 1)
            low = jnp.where(lane4 < BINS - shift, low, high)
        for x in range(4):
            send4[4 * x + y] = low[x : x + 1]

    def stage4(r):
        return pltpu.make_async_remote_copy(
            src_ref=send4.at[(xy + r) % N_XY], dst_ref=recv4.at[xy],
            send_sem=s4_send, recv_sem=s4_recv,
            device_id=xy_peer(r), device_id_type=MESH,
        )

    @pl.loop(1, N_XY)
    def _(r):
        stage4(r).start()

    recv4[xy] = send4[xy]
    hl.wait_send()
    for copy in sq_copies:
        copy.wait_send()
    pltpu.make_async_copy(
        send1.at[pl.ds(0, N_Z - 1)], send1.at[pl.ds(0, N_Z - 1)], s1_send
    ).wait()
    pltpu.make_async_copy(
        send2.at[pl.ds(0, N_XY - 1)], send2.at[pl.ds(0, N_XY - 1)], s2_send
    ).wait()
    pltpu.make_async_copy(
        parts.at[pl.ds(0, N_ZD - 1)], parts.at[pl.ds(0, N_ZD - 1)], s3_send
    ).wait()
    pltpu.make_async_copy(
        send4.at[pl.ds(0, N_XY - 1)], send4.at[pl.ds(0, N_XY - 1)], s4_send
    ).wait()
    pltpu.make_async_copy(
        recv4.at[pl.ds(0, N_XY - 1)], recv4.at[pl.ds(0, N_XY - 1)], s4_recv
    ).wait()
    total = recv4[0]
    for q in range(1, N_XY):
        total += recv4[q]
    out_ref[...] = total * (1.0 / math.sqrt(256 * BINS))


def shards(spectra, valid, lags, drift, block_table):
    f32, bf16, i32 = jnp.float32, jnp.bfloat16, jnp.int32
    table = block_table.reshape(8, 128, 2).transpose(0, 2, 1).reshape(16, 128)
    dma = pltpu.SemaphoreType.DMA
    out = pl.pallas_call(
        kernel,
        out_shape=jax.ShapeDtypeStruct((1, BINS), f32),
        in_specs=[pl.BlockSpec(memory_space=pltpu.HBM)] * 5,
        out_specs=pl.BlockSpec(memory_space=pltpu.VMEM),
        scratch_shapes=[
            pltpu.VMEM((128, BINS), bf16),
            pltpu.VMEM((128, BINS), bf16),
            pltpu.VMEM((384, 128), f32),
            pltpu.VMEM((384, 128), f32),
            pltpu.VMEM((16, 128), i32),
            pltpu.SMEM((16, 128), i32),
            pltpu.SMEM((2,), i32),
            pltpu.VMEM((8, BINS), f32),
            pltpu.VMEM((N_DET, 8, BINS), f32),
            pltpu.VMEM((N_Z, N_XY, 4 * BINS), bf16),
            pltpu.VMEM((N_Z, N_XY, 4 * BINS), bf16),
            pltpu.VMEM((N_XY, 16, 2 * BINS), bf16),
            pltpu.VMEM((N_XY, 16, 2 * BINS), bf16),
            pltpu.VMEM((CHUNKS, 256, 256), bf16),
            pltpu.VMEM((CHUNKS, 256, BINS), f32),
            pltpu.VMEM((CHUNKS, 256, BINS), f32),
            pltpu.VMEM((N_ZD, TILES_OWN, 8, BINS), f32),
            pltpu.VMEM((8, BINS), f32),
            pltpu.VMEM((N_ZD, 8, BINS), f32),
            pltpu.VMEM((16, BINS), f32),
            pltpu.VMEM((N_XY, 1, BINS), f32),
            pltpu.VMEM((N_XY, 1, BINS), f32),
            dma((6,)), dma, dma, dma((3,)), dma((3,)), dma, dma,
            dma, dma, dma, dma, dma, dma,
        ],
        compiler_params=pltpu.CompilerParams(
            collective_id=0, has_side_effects=True, vmem_limit_bytes=32 * 1024 * 1024
        ),
        name="radiometer",
    )(
        spectra.reshape(128, BINS),
        valid,
        lags.reshape(384, 128),
        drift.reshape(384, 128),
        table,
    )
    return out.reshape(BINS)[:PIX_OWN]


def solution(mesh):
    placed = (P("det", "tm", None, None, None), P("tm"), P(), P(), P())
    return jax.shard_map(
        shards, mesh=mesh, in_specs=placed, out_specs=P(("det", "tm")), check_vma=False
    )
```

time: 380 us -> 49.1 us (0.13)
  waiting for transfers between devices: 272 us -> 0 us
  Pallas kernels: 0 us -> 44.4 us
  local copies, waits for them, and re-layouts: 35.6 us -> 4.47 us
  other arithmetic: 19.4 us -> 0 us
  starting transfers between devices: 19 us -> 0 us
  between operations: 15.6 us -> 0.01 us
  blocking collectives: 10.2 us -> 0 us
  loops' own time: 5.79 us -> 0 us
    psum x1 -> x0, waiting for transfers between devices: 258 us -> none  [shards(): summed = lax.psum(sky_map, ('det', 'tm'))]
    pallas_call x0 -> x1, Pallas kernels: none -> 44.4 us  [shards(): pl.pallas_call(kernel, out_shape=jax.ShapeDtypeStruct((1, BINS), f32), in...]
    gather x10 -> x0, local copies, waits for them, and re-layouts: 27.2 us -> none  [the longest x4 12.6 us: one_item(): jnp.take(lags, pixels)]
    all_to_all x1 -> x0, starting transfers between devices: 14.9 us -> none  [shards(): lax.all_to_all(outgoing, 'tm', split_axis=0, concat_axis=2, tiled=True)]
    all_to_all x1 -> x0, waiting for transfers between devices: 14.8 us -> none  [shards(): lax.all_to_all(outgoing, 'tm', split_axis=0, concat_axis=2, tiled=True)]
    psum x1 -> x0, blocking collectives: 10.2 us -> none  [shards(): powers = lax.psum(stacked, 'det') / (band_total * band_width) + 1e-06]
    another operation x1 -> x0, loops' own time: 5.79 us -> none  [shards(): partials = lax.map(one_item, (received[0], item_bands, item_tiles))]
    mul x12 -> x0, other arithmetic: 5.09 us -> none  [the longest x4 2.54 us: one_item(): tile_ids[:, None] * PT + jnp.arange(PT, dtype=jnp.int32)[None, :]]
  transfers between devices with their start and end apart: 3 -> 0, of which waited for: 2 -> 0; matrix products, arithmetic and copies ran while one was open for 1% -> 0% of each run, Pallas kernels for 0% -> 0%
where the time goes in v1:
time: 49.1 us; the launch traced here: 48.9 us
  Pallas kernels  44.4 us (90%)
  local copies, waits for them, and re-layouts  4.47 us (9%)
    pallas_call x1, Pallas kernels, shards(): pl.pallas_call(kernel, out_shape=jax.ShapeDtypeStruct((1, BINS), f32), in...  44.4 us
    unnamed x10, local copies, waits for them, and re-layouts  3.96 us

profile of v1, /device:TPU:1, one launch (start us, length us, event | category | flops | bytes accessed | tf_op | source)
XLA Modules:
  0.0 48.9 jit_solution(6427474132749937547)
XLA Ops:
  0.0 0.0 copy-start.4
  0.0 0.7 %copy-done.4 = s32[2]{0:T(128)S(1)} copy-done((s32[2]{0:T(128)S(1)}, s32[2]{0:T(128)}, u32[]{:S(2)}) %copy-start.4) | copy-done | bytes 32
  0.7 0.0 copy-start
  0.7 0.9 %copy-done = f32[49152]{0:T(1024)S(1)} copy-done((f32[49152]{0:T(1024)S(1)}, f32[49152]{0:T(1024)}, u32[]{:S(2)}) %copy-start) | copy-done | bytes 196632
  1.6 0.0 copy-start.1
  1.6 0.9 %copy-done.1 = f32[49152]{0:T(1024)S(1)} copy-done((f32[49152]{0:T(1024)S(1)}, f32[49152]{0:T(1024)}, u32[]{:S(2)}) %copy-start.1) | copy-done | bytes 196632
  2.5 0.0 copy-start.2
  2.5 0.8 %copy-done.2 = bf16[1,2,32,2,128]{4,3,2,1,0:T(2,128)(2,1)S(1)} copy-done((bf16[1,2,32,2,128]{4,3,2,1,0:T(2,128)(2,1)S(1)}, bf16[1,2,32,2,128]{4,3,2,1,0:T(2,128)(2,1)}, u32[]{:S(2)}) %copy-start.2) | copy-done | bytes 32792
  3.3 0.0 copy-start.3
  3.3 0.7 %copy-done.3 = s32[1024,2]{0,1:T(2,128)S(1)} copy-done((s32[1024,2]{0,1:T(2,128)S(1)}, s32[1024,2]{0,1:T(2,128)}, u32[]{:S(2)}) %copy-start.3) | copy-done | bytes 8216
  4.0 44.4 %radiometer.1 = f32[1,128]{1,0:T(1,128)S(1)} custom-call(bf16[128,128]{1,0:T(8,128)(2,1)S(1)} %bitcast.12, s32[2]{0:T(128)S(1)} %copy-done.4, f32[384,128]{1,0:T(8,128)S(1)} %bitcast.10, f32[384,128]{1,0:T(8,128)S(1)} %bitcast.11, s32[16,128]{1,0:T(8,128)S(1)} %bitcast.13), custom_call_target="tpu_custom_call" | custom-call | tf_op jit(solution)/shard_map/radiometer/pallas_call | solution.py:323
  48.3 0.5 %slice_bitcast_fusion = f32[96]{0:T(128)} fusion(f32[1,128]{1,0:T(1,128)S(1)} %radiometer.1), kind=kLoop, calls=%fused_computation | loop fusion | bytes 768 | tf_op jit(solution)/shard_map/slice | solution.py:365
Async XLA Ops:
  0.0 0.7 %copy-start.4 = (s32[2]{0:T(128)S(1)}, s32[2]{0:T(128)}, u32[]{:S(2)}) copy-start(s32[2]{0:T(128)} %valid_hbm.1) | copy-start | bytes 28
  0.7 0.9 %copy-start = (f32[49152]{0:T(1024)S(1)}, f32[49152]{0:T(1024)}, u32[]{:S(2)}) copy-start(f32[49152]{0:T(1024)} %param.7) | copy-start | bytes 589828
  1.6 0.9 %copy-start.1 = (f32[49152]{0:T(1024)S(1)}, f32[49152]{0:T(1024)}, u32[]{:S(2)}) copy-start(f32[49152]{0:T(1024)} %param.8) | copy-start | bytes 589828
  2.5 0.8 %copy-start.2 = (bf16[1,2,32,2,128]{4,3,2,1,0:T(2,128)(2,1)S(1)}, bf16[1,2,32,2,128]{4,3,2,1,0:T(2,128)(2,1)}, u32[]{:S(2)}) copy-start(bf16[1,2,32,2,128]{4,3,2,1,0:T(2,128)(2,1)} %param.5) | copy-start | bytes 98308
  3.3 0.7 %copy-start.3 = (s32[1024,2]{0,1:T(2,128)S(1)}, s32[1024,2]{0,1:T(2,128)}, u32[]{:S(2)}) copy-start(s32[1024,2]{0,1:T(2,128)} %param.9) | copy-start | bytes 24580

commit v2 on v1

v2 whole, which is shorter than its diff:
```python
import math

import jax
import jax.numpy as jnp
from jax import lax
from jax.experimental import pallas as pl
from jax.experimental.pallas import tpu as pltpu
from jax.sharding import PartitionSpec as P

MESH = pl.DeviceIdType.MESH

N_DET = 4
N_TM = 128
N_Z = 8
N_XY = 16
N_ZH = 16
N_XYK = 32
BINS = 128
BANDS = 32
TILES_OWN = 3
TILES_SUM = 6
PIX_OWN = 96
CHUNKS = 8

SIN = [(-1.0) ** n * (2 * math.pi) ** (2 * n + 1) / math.factorial(2 * n + 1) for n in range(6)]
COS = [(-1.0) ** n * (2 * math.pi) ** (2 * n) / math.factorial(2 * n) for n in range(7)]


def horner(coefficients, x):
    total = jnp.full_like(x, coefficients[-1])
    for c in coefficients[-2::-1]:
        total = total * x + c
    return total


def cos_sin(turns):
    half = jnp.floor(turns * 2.0 + 0.5)
    r = turns - half * 0.5
    sign = 1.0 - 2.0 * (half - 2.0 * jnp.floor(half * 0.5))
    square = r * r
    return sign * horner(COS, square), sign * r * horner(SIN, square)


def iota(shape, dim):
    return lax.broadcasted_iota(jnp.int32, shape, dim)


def kernel(
    spec_hbm, valid_hbm, lags_hbm, drift_hbm, table_hbm, out_ref,
    own_v, other_v, lags_v, drift_v, table_v, table_s, valid_s,
    squares, squares_all, send2, recv2,
    kmat, rot_cos, rot_sin, masks, part, parts, folded, send4, recv4,
    local_sem, hl_send, hl_recv, sq_send, sq_recv,
    s2_send, s2_recv, s3_send, s3_recv, s4_send, s4_recv, plane_sem, space_sem,
):
    det = lax.axis_index("det")
    tm = lax.axis_index("tm")
    k, h = det // 2, det % 2
    z, xy = tm // N_XY, tm % N_XY
    x, y = xy // 4, xy % 4
    yk = y * 2 + k
    zh = z * 2 + h
    xyk = xy * 2 + k

    def z_peer(r):
        return (det, (z + r) % N_Z * N_XY + xy)

    def x_peer(r):
        return (det, z * N_XY + (x + r) % 4 * 4 + y)

    def y_peer(r):
        p = (yk + r) % 8
        return (p % 2 * 2 + h, z * N_XY + x * 4 + p // 2)

    def zh_peer(r):
        p = (zh + r) % N_ZH
        return (k * 2 + p % 2, p // 2 * N_XY + xy)

    def xyk_peer(r):
        p = (xyk + r) % N_XYK
        return (p % 2 * 2 + h, z * N_XY + p // 2)

    core_peer = (k * 2 + 1 - h, tm)
    across_peer = (3 - det, tm)

    barrier = pltpu.get_barrier_semaphore()

    def tell(semaphore, peer):
        pl.semaphore_signal(semaphore, inc=1, device_id=peer, device_id_type=MESH)

    @pl.loop(1, N_Z)
    def _(r):
        tell(barrier, z_peer(r))

    @pl.loop(1, 8)
    def _(r):
        tell(barrier, y_peer(r))

    @pl.loop(1, 4)
    def _(r):
        tell(barrier, x_peer(r))

    tell(barrier, core_peer)
    tell(barrier, across_peer)

    loads = [
        pltpu.make_async_copy(src, dst, local_sem.at[n])
        for n, (src, dst) in enumerate(
            [
                (spec_hbm, own_v), (table_hbm, table_s), (table_hbm, table_v),
                (valid_hbm, valid_s), (lags_hbm, lags_v), (drift_hbm, drift_v),
            ]
        )
    ]
    for load in loads:
        load.start()
    loads[0].wait()

    own = own_v[...].astype(jnp.float32)
    sq = own * own
    row8 = iota((8, BINS), 0)
    seg0 = jnp.sum(sq[:64], axis=0, keepdims=True)
    seg1 = jnp.sum(sq[64:], axis=0, keepdims=True)
    sums = jnp.where(row8 == 0, seg0, jnp.where(row8 == 1, seg1, 0.0))
    squares[...] = sums
    squares_all[det] = sums

    pl.semaphore_wait(barrier, 7 + 7 + 3 + 2)

    hl = pltpu.make_async_remote_copy(
        src_ref=own_v, dst_ref=other_v, send_sem=hl_send, recv_sem=hl_recv,
        device_id=((det + 2) % N_DET, tm), device_id_type=MESH,
    )
    hl.start()
    sq_copies = [
        pltpu.make_async_remote_copy(
            src_ref=squares, dst_ref=squares_all.at[det],
            send_sem=sq_send.at[r - 1], recv_sem=sq_recv.at[r - 1],
            device_id=((det + r) % N_DET, tm), device_id_type=MESH,
        )
        for r in range(1, N_DET)
    ]
    for copy in sq_copies:
        copy.start()

    @pl.loop(1, 4)
    def _(r):
        tell(plane_sem, x_peer(r))

    tell(plane_sem, core_peer)
    for load in loads[1:]:
        load.wait()

    bands = table_v[...].astype(jnp.float32)
    target = iota((4 * N_TM, BINS), 0)
    wanted = iota((4 * N_XY, BINS), 1) == (
        8 * (iota((4 * N_XY, BINS), 0) // 4) + 4 * h + 2 * k
    )
    picks = []
    for dz in range(N_Z):
        column = jnp.where(wanted, bands[2 * dz : 2 * dz + 1], 0.0)
        picks.append(jnp.sum(column, axis=1, keepdims=True))
    pick = (jnp.concatenate(picks, axis=0) - (BANDS * h).astype(jnp.float32)) * 2.0
    segment = (target[:, 0:1] // 2 % 2).astype(jnp.float32) * 64.0
    is_imag = target[:, 0:1] % 2
    source = iota((4 * N_TM, BINS), 1).astype(jnp.float32)
    chosen = jnp.where(source == pick + segment, 1.0, 0.0)
    pick_real = jnp.where(is_imag == 0, chosen, 0.0).astype(jnp.bfloat16)
    pick_imag = jnp.where(is_imag == 1, chosen, 0.0).astype(jnp.bfloat16)
    pick = jnp.concatenate([pick_real, pick_imag], axis=1)

    pl.semaphore_wait(plane_sem, 4)

    @pl.loop(1, N_Z)
    def _(r):
        tell(space_sem, z_peer(r))

    hl.wait_recv()
    other = other_v[...].astype(jnp.float32)
    own_up = pltpu.roll(own, BINS - 1, 0)
    other_up = pltpu.roll(other, BINS - 1, 0)
    sign = (1 - 2 * k).astype(jnp.float32)
    cross_real = own * other + own_up * other_up
    cross_imag = (own * other_up - own_up * other) * sign
    for copy in sq_copies:
        copy.wait_recv()
    total = lambda a: jnp.sum(a, axis=1, keepdims=True) / 8192.0 + 1e-06
    power_h = total(squares_all[0] + squares_all[1])
    power_l = total(squares_all[2] + squares_all[3])
    flags = jnp.where(iota((8, 1), 0) == 0, valid_s[0], valid_s[1]).astype(jnp.float32)
    weight = flags / (power_h * power_l)
    weights = jnp.where(iota((BINS, 1), 0) < 64, weight[0:1], weight[1:2])
    cross = jnp.concatenate([cross_real * weights, cross_imag * weights], axis=0)
    rows = jnp.dot(pick, cross.astype(jnp.bfloat16), preferred_element_type=jnp.float32)
    send2.reshape(4 * N_TM, BINS)[...] = rows.astype(jnp.bfloat16)

    pl.semaphore_wait(space_sem, N_Z - 1)

    def stage2(r):
        to = (tm + r) % N_TM
        return pltpu.make_async_remote_copy(
            src_ref=send2.at[to], dst_ref=recv2.at[tm],
            send_sem=s2_send, recv_sem=s2_recv,
            device_id=(det, to), device_id_type=MESH,
        )

    @pl.loop(1, N_TM)
    def _(r):
        stage2(r).start()

    recv2[tm] = send2[tm]

    g = table_s[2 * z, 8 * xy + 4 * h + 2 * k]
    g_f = g.astype(jnp.float32)
    first = [table_s[2 * z + 1, 8 * xy + 4 * h + 2 * k + n] for n in range(2)]
    col16 = iota((16, BINS), 0)
    col8 = iota((8, BINS), 0)

    @pl.loop(0, CHUNKS)
    def _(ch):
        tile = jnp.where(ch < 4, first[0], first[1])
        lag = lags_v[pl.ds(4 * tile + ch % 4, 1), :]
        ca, sa = cos_sin((g * BINS + 16 * col8).astype(jnp.float32) * lag)
        cb, sb = cos_sin(col16.astype(jnp.float32) * lag)
        for a in range(8):
            c1, s1 = ca[a : a + 1], sa[a : a + 1]
            cosine = (c1 * cb - s1 * sb).astype(jnp.bfloat16)
            sine = (s1 * cb + c1 * sb).astype(jnp.bfloat16)
            kmat[ch, 16 * a : 16 * a + 16, 0:BINS] = cosine
            kmat[ch, 16 * a : 16 * a + 16, BINS:] = -sine
            kmat[ch, BINS + 16 * a : BINS + 16 * a + 16, 0:BINS] = sine
            kmat[ch, BINS + 16 * a : BINS + 16 * a + 16, BINS:] = cosine

    time_a = (16 * col16).astype(jnp.float32) - 127.5
    time_b = (2 * (col16 % 8) + col16 // 8).astype(jnp.float32)
    scale = (g_f + 0.5) * (1.0 / (64 * 256))

    @pl.loop(0, CHUNKS)
    def _(ch):
        tile = jnp.where(ch < 4, first[0], first[1])
        rate = drift_v[pl.ds(4 * tile + ch % 4, 1), :] * scale
        ca, sa = cos_sin(time_a * rate)
        cb, sb = cos_sin(time_b * rate)
        for a in range(16):
            c1, s1 = ca[a : a + 1], sa[a : a + 1]
            cosine = c1 * cb - s1 * sb
            sine = s1 * cb + c1 * sb
            for s in range(2):
                at = s * N_TM + 8 * a
                rot_cos[ch, at : at + 8, :] = cosine[8 * s : 8 * s + 8]
                rot_sin[ch, at : at + 8, :] = sine[8 * s : 8 * s + 8]

    @pl.loop(0, N_ZH)
    def _(p):
        at = 8 * xy + 4 * (p % 2) + 2 * k
        t0 = table_s[2 * (p // 2) + 1, at]
        t1 = table_s[2 * (p // 2) + 1, at + 1]
        tiles = jnp.where(row8 < 4, t0, t1)
        for j in range(TILES_SUM):
            tile = 24 * (j // 3 * 2 + h) + 3 * z + j % 3
            masks[p, j] = jnp.where(tiles == tile, 1.0, 0.0)

    o, n = iota((256, 512), 0), iota((256, 512), 1)
    want = 4 * (o % N_TM) + 2 * (o // N_TM)
    perms = [
        jnp.where(n == want + c, 1.0, 0.0).astype(jnp.bfloat16) for c in range(2)
    ]

    pltpu.make_async_copy(
        recv2.at[pl.ds(0, N_TM - 1)], recv2.at[pl.ds(0, N_TM - 1)], s2_recv
    ).wait()

    got = recv2.reshape(4 * N_TM, BINS)[...]
    slab = jnp.concatenate(
        [jnp.dot(p, got, preferred_element_type=jnp.float32) for p in perms], axis=1
    ).astype(jnp.bfloat16)

    for ch in range(CHUNKS):
        product = jnp.dot(slab, kmat[ch], preferred_element_type=jnp.float32)
        turned = rot_cos[ch] * product[:, :BINS] - rot_sin[ch] * product[:, BINS:]
        part[ch : ch + 1, :] = jnp.sum(turned, axis=0, keepdims=True)

    def stage3(r):
        return pltpu.make_async_remote_copy(
            src_ref=part, dst_ref=parts.at[zh],
            send_sem=s3_send, recv_sem=s3_recv,
            device_id=zh_peer(r), device_id_type=MESH,
        )

    @pl.loop(1, N_ZH)
    def _(r):
        stage3(r).start()

    parts[zh] = part[...]
    pltpu.make_async_copy(
        parts.at[pl.ds(0, N_ZH - 1)], parts.at[pl.ds(0, N_ZH - 1)], s3_recv
    ).wait()

    sums = [jnp.zeros((8, BINS), jnp.float32) for _ in range(TILES_SUM)]
    for p in range(N_ZH):
        terms = parts[p]
        for j in range(TILES_SUM):
            sums[j] += terms * masks[p, j]
    for j in range(TILES_SUM):
        at = 16 * (j // 3) + 4 * (j % 3)
        folded[at : at + 4, :] = sums[j][0:4] + sums[j][4:8]
    lane4 = iota((4, BINS), 1)
    for q in range(2):
        rows = [folded[pl.ds(16 * q + i, 4, stride=3), :] for i in range(3)]
        for j in range(4):
            at, shift = 96 * j // BINS, 96 * j % BINS
            low = pltpu.roll(rows[at], BINS - shift, 1) if shift else rows[at]
            if BINS - shift < PIX_OWN:
                high = pltpu.roll(rows[at + 1], BINS - shift, 1)
                low = jnp.where(lane4 < BINS - shift, low, high)
            for i in range(4):
                send4[(4 * i + j) * 2 + q] = low[i : i + 1]

    def stage4(r):
        return pltpu.make_async_remote_copy(
            src_ref=send4.at[(xyk + r) % N_XYK], dst_ref=recv4.at[xyk],
            send_sem=s4_send, recv_sem=s4_recv,
            device_id=xyk_peer(r), device_id_type=MESH,
        )

    @pl.loop(1, N_XYK)
    def _(r):
        stage4(r).start()

    recv4[xyk] = send4[xyk]
    hl.wait_send()
    for copy in sq_copies:
        copy.wait_send()
    pltpu.make_async_copy(
        send2.at[pl.ds(0, N_TM - 1)], send2.at[pl.ds(0, N_TM - 1)], s2_send
    ).wait()
    pltpu.make_async_copy(
        parts.at[pl.ds(0, N_ZH - 1)], parts.at[pl.ds(0, N_ZH - 1)], s3_send
    ).wait()
    pltpu.make_async_copy(
        send4.at[pl.ds(0, N_XYK - 1)], send4.at[pl.ds(0, N_XYK - 1)], s4_send
    ).wait()
    pltpu.make_async_copy(
        recv4.at[pl.ds(0, N_XYK - 1)], recv4.at[pl.ds(0, N_XYK - 1)], s4_recv
    ).wait()
    total = recv4[0]
    for q in range(1, N_XYK):
        total += recv4[q]
    out_ref[...] = total * (1.0 / math.sqrt(256 * BINS))


def shards(spectra, valid, lags, drift, block_table):
    f32, bf16, i32 = jnp.float32, jnp.bfloat16, jnp.int32
    table = block_table.reshape(8, 128, 2).transpose(0, 2, 1).reshape(16, 128)
    dma = pltpu.SemaphoreType.DMA
    out = pl.pallas_call(
        kernel,
        out_shape=jax.ShapeDtypeStruct((1, BINS), f32),
        in_specs=[pl.BlockSpec(memory_space=pltpu.HBM)] * 5,
        out_specs=pl.BlockSpec(memory_space=pltpu.VMEM),
        scratch_shapes=[
            pltpu.VMEM((128, BINS), bf16),
            pltpu.VMEM((128, BINS), bf16),
            pltpu.VMEM((384, 128), f32),
            pltpu.VMEM((384, 128), f32),
            pltpu.VMEM((16, 128), i32),
            pltpu.SMEM((16, 128), i32),
            pltpu.SMEM((2,), i32),
            pltpu.VMEM((8, BINS), f32),
            pltpu.VMEM((N_DET, 8, BINS), f32),
            pltpu.VMEM((N_TM, 4, BINS), bf16),
            pltpu.VMEM((N_TM, 4, BINS), bf16),
            pltpu.VMEM((CHUNKS, 256, 256), bf16),
            pltpu.VMEM((CHUNKS, 256, BINS), f32),
            pltpu.VMEM((CHUNKS, 256, BINS), f32),
            pltpu.VMEM((N_ZH, TILES_SUM, 8, BINS), f32),
            pltpu.VMEM((8, BINS), f32),
            pltpu.VMEM((N_ZH, 8, BINS), f32),
            pltpu.VMEM((32, BINS), f32),
            pltpu.VMEM((N_XYK, 1, BINS), f32),
            pltpu.VMEM((N_XYK, 1, BINS), f32),
            dma((6,)), dma, dma, dma((3,)), dma((3,)), dma, dma, dma, dma, dma, dma,
            pltpu.SemaphoreType.REGULAR, pltpu.SemaphoreType.REGULAR,
        ],
        compiler_params=pltpu.CompilerParams(
            collective_id=0, has_side_effects=True, vmem_limit_bytes=60 * 1024 * 1024
        ),
        name="radiometer",
    )(
        spectra.reshape(128, BINS),
        valid,
        lags.reshape(384, 128),
        drift.reshape(384, 128),
        table,
    )
    return out.reshape(BINS)[:PIX_OWN]


def solution(mesh):
    placed = (P("det", "tm", None, None, None), P("tm"), P(), P(), P())
    return jax.shard_map(
        shards, mesh=mesh, in_specs=placed, out_specs=P(("det", "tm")), check_vma=False
    )
```

time: 49.1 us -> 42 us (0.86)
  Pallas kernels: 44.4 us -> 40.6 us
  local copies, waits for them, and re-layouts: 4.47 us -> 1.19 us
    unnamed x10 -> x0, local copies, waits for them, and re-layouts: 3.96 us -> none
    pallas_call x1, Pallas kernels: 44.4 us -> 40.6 us  [shards(): pl.pallas_call(kernel, out_shape=jax.ShapeDtypeStruct((1, BINS), f32), in...]
    slice x1, local copies, waits for them, and re-layouts: 0.51 us -> 1.19 us  [shards(): return out.reshape(BINS)[:PIX_OWN]]
where the time goes in v2:
time: 42 us; the launch traced here: 41.8 us
  Pallas kernels  40.6 us (97%)
  local copies, waits for them, and re-layouts  1.19 us (3%)
    pallas_call x1, Pallas kernels, shards(): pl.pallas_call(kernel, out_shape=jax.ShapeDtypeStruct((1, BINS), f32), in...  40.6 us
    slice x1, local copies, waits for them, and re-layouts, shards(): return out.reshape(BINS)[:PIX_OWN]  1.19 us

profile of v2, /device:TPU:1, one launch (start us, length us, event | category | flops | bytes accessed | tf_op | source)
XLA Modules:
  0.0 41.8 jit_solution(5783403372342324898)
XLA Ops:
  0.0 40.6 %radiometer.1 = f32[1,128]{1,0:T(1,128)} custom-call(bf16[128,128]{1,0:T(8,128)(2,1)} %bitcast.12, s32[2]{0:T(128)} %valid_hbm.1, f32[384,128]{1,0:T(8,128)} %bitcast.10, f32[384,128]{1,0:T(8,128)} %bitcast.11, s32[16,128]{1,0:T(8,128)} %bitcast.13), custom_call_target="tpu_custom_call" | custom-call | tf_op jit(solution)/shard_map/radiometer/pallas_call | solution.py:356
  40.6 1.2 %slice_bitcast_fusion = f32[96]{0:T(128)} fusion(f32[1,128]{1,0:T(1,128)} %radiometer.1), kind=kLoop, calls=%fused_computation | loop fusion | bytes 768 | tf_op jit(solution)/shard_map/slice | solution.py:396

commit v3 on v2

--- a/solution.py
+++ b/solution.py
@@ -80,6 +80,13 @@
         p = (xyk + r) % N_XYK
         return (p % 2 * 2 + h, z * N_XY + p // 2)
 
+    step = 2 * k - 1
+
+    def chip_at(distance):
+        chip = (yk + step * distance + 8) % 8
+        return chip % 2 * 2 + h, chip // 2
+
+    sent_to = [chip_at(j) for j in range(4)]
     core_peer = (k * 2 + 1 - h, tm)
     across_peer = (3 - det, tm)
 
@@ -125,7 +132,35 @@
     squares[...] = sums
     squares_all[det] = sums
 
+    for load in loads[1:]:
+        load.wait()
+
+    bands = table_v[...].astype(jnp.float32)
+    target = iota((4 * N_TM, BINS), 0)
+    row = iota((4 * N_XY, BINS), 0)
+    chip = (yk + step * (row // 4 % 4) + 8) % 8
+    at = 32 * (row // 16) + 8 * (chip // 2) + 2 * (chip % 2) + 4 * h
+    wanted = iota((4 * N_XY, BINS), 1) == at
+    picks = []
+    for dz in range(N_Z):
+        column = jnp.where(wanted, bands[2 * dz : 2 * dz + 1], 0.0)
+        picks.append(jnp.sum(column, axis=1, keepdims=True))
+    pick = (jnp.concatenate(picks, axis=0) - (BANDS * h).astype(jnp.float32)) * 2.0
+    segment = (target[:, 0:1] // 2 % 2).astype(jnp.float32) * 64.0
+    is_imag = target[:, 0:1] % 2
+    source = iota((4 * N_TM, BINS), 1).astype(jnp.float32)
+    chosen = jnp.where(source == pick + segment, 1.0, 0.0)
+    pick_real = jnp.where(is_imag == 0, chosen, 0.0).astype(jnp.bfloat16)
+    pick_imag = jnp.where(is_imag == 1, chosen, 0.0).astype(jnp.bfloat16)
+    pick = jnp.concatenate([pick_real, pick_imag], axis=1)
+
     pl.semaphore_wait(barrier, 7 + 7 + 3 + 2)
+
+    @pl.loop(1, 4)
+    def _(r):
+        tell(plane_sem, x_peer(r))
+
+    tell(plane_sem, core_peer)
 
     hl = pltpu.make_async_remote_copy(
         src_ref=own_v, dst_ref=other_v, send_sem=hl_send, recv_sem=hl_recv,
@@ -143,37 +178,11 @@
     for copy in sq_copies:
         copy.start()
 
-    @pl.loop(1, 4)
-    def _(r):
-        tell(plane_sem, x_peer(r))
-
-    tell(plane_sem, core_peer)
-    for load in loads[1:]:
-        load.wait()
-
-    bands = table_v[...].astype(jnp.float32)
-    target = iota((4 * N_TM, BINS), 0)
-    wanted = iota((4 * N_XY, BINS), 1) == (
-        8 * (iota((4 * N_XY, BINS), 0) // 4) + 4 * h + 2 * k
-    )
-    picks = []
-    for dz in range(N_Z):
-        column = jnp.where(wanted, bands[2 * dz : 2 * dz + 1], 0.0)
-        picks.append(jnp.sum(column, axis=1, keepdims=True))
-    pick = (jnp.concatenate(picks, axis=0) - (BANDS * h).astype(jnp.float32)) * 2.0
-    segment = (target[:, 0:1] // 2 % 2).astype(jnp.float32) * 64.0
-    is_imag = target[:, 0:1] % 2
-    source = iota((4 * N_TM, BINS), 1).astype(jnp.float32)
-    chosen = jnp.where(source == pick + segment, 1.0, 0.0)
-    pick_real = jnp.where(is_imag == 0, chosen, 0.0).astype(jnp.bfloat16)
-    pick_imag = jnp.where(is_imag == 1, chosen, 0.0).astype(jnp.bfloat16)
-    pick = jnp.concatenate([pick_real, pick_imag], axis=1)
-
     pl.semaphore_wait(plane_sem, 4)
 
-    @pl.loop(1, N_Z)
-    def _(r):
-        tell(space_sem, z_peer(r))
+    for distance in (1, 3, -2):
+        d, chip_y = chip_at(distance)
+        tell(space_sem, (d, z * N_XY + x * 4 + chip_y))
 
     hl.wait_recv()
     other = other_v[...].astype(jnp.float32)
@@ -194,21 +203,27 @@
     rows = jnp.dot(pick, cross.astype(jnp.bfloat16), preferred_element_type=jnp.float32)
     send2.reshape(4 * N_TM, BINS)[...] = rows.astype(jnp.bfloat16)
 
-    pl.semaphore_wait(space_sem, N_Z - 1)
-
-    def stage2(r):
-        to = (tm + r) % N_TM
+    zx = z * 4 + x
+
+    def stage2(to_zx, j):
+        d, chip_y = sent_to[j]
         return pltpu.make_async_remote_copy(
-            src_ref=send2.at[to], dst_ref=recv2.at[tm],
+            src_ref=send2.at[4 * to_zx + j], dst_ref=recv2.at[tm],
             send_sem=s2_send, recv_sem=s2_recv,
-            device_id=(det, to), device_id_type=MESH,
+            device_id=(d, 4 * to_zx + chip_y), device_id_type=MESH,
         )
 
-    @pl.loop(1, N_TM)
-    def _(r):
-        stage2(r).start()
-
-    recv2[tm] = send2[tm]
+    pl.semaphore_wait(space_sem, 3)
+
+    for j in range(1, 4):
+        stage2(zx, j).start()
+
+    @pl.loop(1, 32)
+    def _(r):
+        for j in range(4):
+            stage2((zx + r) % 32, j).start()
+
+    recv2[tm] = send2[4 * zx]
 
     g = table_s[2 * z, 8 * xy + 4 * h + 2 * k]
     g_f = g.astype(jnp.float32)
@@ -355,7 +370,7 @@
     dma = pltpu.SemaphoreType.DMA
     out = pl.pallas_call(
         kernel,
-        out_shape=jax.ShapeDtypeStruct((1, BINS), f32),
+        out_shape=pltpu.VMEM((1, BINS), f32),
         in_specs=[pl.BlockSpec(memory_space=pltpu.HBM)] * 5,
         out_specs=pl.BlockSpec(memory_space=pltpu.VMEM),
         scratch_shapes=[

time: 42 us -> 39.8 us (0.948)
  Pallas kernels: 40.6 us -> 39.1 us
  local copies, waits for them, and re-layouts: 1.19 us -> 0.51 us
    pallas_call x1, Pallas kernels: 40.6 us -> 39.1 us  [shards(): pl.pallas_call(kernel, out_shape=pltpu.VMEM((1, BINS), f32), in_specs=[pl...]
    slice x1, local copies, waits for them, and re-layouts: 1.19 us -> 0.51 us  [shards(): return out.reshape(BINS)[:PIX_OWN]]
where the time goes in v3:
time: 39.8 us; the launch traced here: 39.6 us
  Pallas kernels  39.1 us (98%)
  local copies, waits for them, and re-layouts  0.51 us (1%)
    pallas_call x1, Pallas kernels, shards(): pl.pallas_call(kernel, out_shape=pltpu.VMEM((1, BINS), f32), in_specs=[pl...  39.1 us

profile of v3, /device:TPU:1, one launch (start us, length us, event | category | flops | bytes accessed | tf_op | source)
XLA Modules:
  0.0 39.6 jit_solution(11018932725154344712)
XLA Ops:
  0.0 39.1 %radiometer.1 = f32[1,128]{1,0:T(1,128)S(1)} custom-call(bf16[128,128]{1,0:T(8,128)(2,1)} %bitcast.12, s32[2]{0:T(128)} %valid_hbm.1, f32[384,128]{1,0:T(8,128)} %bitcast.10, f32[384,128]{1,0:T(8,128)} %bitcast.11, s32[16,128]{1,0:T(8,128)} %bitcast.13), custom_call_target="tpu_custom_call" | custom-call | tf_op jit(solution)/shard_map/radiometer/pallas_call | solution.py:371
  39.1 0.5 %slice_bitcast_fusion = f32[96]{0:T(128)} fusion(f32[1,128]{1,0:T(1,128)S(1)} %radiometer.1), kind=kLoop, calls=%fused_computation | loop fusion | bytes 768 | tf_op jit(solution)/shard_map/slice | solution.py:411

commit v4 on v3

--- a/solution.py
+++ b/solution.py
@@ -55,36 +55,37 @@
 ):
     det = lax.axis_index("det")
     tm = lax.axis_index("tm")
-    k, h = det // 2, det % 2
-    z, xy = tm // N_XY, tm % N_XY
-    x, y = xy // 4, xy % 4
+    div, rem = lax.div, lax.rem
+    k, h = div(det, 2), rem(det, 2)
+    z, xy = div(tm, N_XY), rem(tm, N_XY)
+    x, y = div(xy, 4), rem(xy, 4)
     yk = y * 2 + k
     zh = z * 2 + h
     xyk = xy * 2 + k
 
     def z_peer(r):
-        return (det, (z + r) % N_Z * N_XY + xy)
+        return (det, rem(z + r, N_Z) * N_XY + xy)
 
     def x_peer(r):
-        return (det, z * N_XY + (x + r) % 4 * 4 + y)
+        return (det, z * N_XY + rem(x + r, 4) * 4 + y)
 
     def y_peer(r):
-        p = (yk + r) % 8
-        return (p % 2 * 2 + h, z * N_XY + x * 4 + p // 2)
+        p = rem(yk + r, 8)
+        return (rem(p, 2) * 2 + h, z * N_XY + x * 4 + div(p, 2))
 
     def zh_peer(r):
-        p = (zh + r) % N_ZH
-        return (k * 2 + p % 2, p // 2 * N_XY + xy)
+        p = rem(zh + r, N_ZH)
+        return (k * 2 + rem(p, 2), div(p, 2) * N_XY + xy)
 
     def xyk_peer(r):
-        p = (xyk + r) % N_XYK
-        return (p % 2 * 2 + h, z * N_XY + p // 2)
+        p = rem(xyk + r, N_XYK)
+        return (rem(p, 2) * 2 + h, z * N_XY + div(p, 2))
 
     step = 2 * k - 1
 
     def chip_at(distance):
-        chip = (yk + step * distance + 8) % 8
-        return chip % 2 * 2 + h, chip // 2
+        chip = rem(yk + step * distance + 8, 8)
+        return rem(chip, 2) * 2 + h, div(chip, 2)
 
     sent_to = [chip_at(j) for j in range(4)]
     core_peer = (k * 2 + 1 - h, tm)
@@ -164,14 +165,14 @@
 
     hl = pltpu.make_async_remote_copy(
         src_ref=own_v, dst_ref=other_v, send_sem=hl_send, recv_sem=hl_recv,
-        device_id=((det + 2) % N_DET, tm), device_id_type=MESH,
+        device_id=(rem(det + 2, N_DET), tm), device_id_type=MESH,
     )
     hl.start()
     sq_copies = [
         pltpu.make_async_remote_copy(
             src_ref=squares, dst_ref=squares_all.at[det],
             send_sem=sq_send.at[r - 1], recv_sem=sq_recv.at[r - 1],
-            device_id=((det + r) % N_DET, tm), device_id_type=MESH,
+            device_id=(rem(det + r, N_DET), tm), device_id_type=MESH,
         )
         for r in range(1, N_DET)
     ]
@@ -220,8 +221,9 @@
 
     @pl.loop(1, 32)
     def _(r):
+        to_zx = rem(zx + r, 32)
         for j in range(4):
-            stage2((zx + r) % 32, j).start()
+            stage2(to_zx, j).start()
 
     recv2[tm] = send2[4 * zx]
 
@@ -333,7 +335,7 @@
 
     def stage4(r):
         return pltpu.make_async_remote_copy(
-            src_ref=send4.at[(xyk + r) % N_XYK], dst_ref=recv4.at[xyk],
+            src_ref=send4.at[rem(xyk + r, N_XYK)], dst_ref=recv4.at[xyk],
             send_sem=s4_send, recv_sem=s4_recv,
             device_id=xyk_peer(r), device_id_type=MESH,
         )
@@ -358,9 +360,8 @@
     pltpu.make_async_copy(
         recv4.at[pl.ds(0, N_XYK - 1)], recv4.at[pl.ds(0, N_XYK - 1)], s4_recv
     ).wait()
-    total = recv4[0]
-    for q in range(1, N_XYK):
-        total += recv4[q]
+    pieces = recv4.reshape(N_XYK, BINS)[...]
+    total = jnp.sum(pieces, axis=0, keepdims=True)
     out_ref[...] = total * (1.0 / math.sqrt(256 * BINS))
 
 

time: 39.8 us -> 39.6 us (level)
  no operation moved by 1% of the time
where the time goes in v4:
time: 39.6 us; the launch traced here: 39.5 us
  Pallas kernels  38.9 us (98%)
  local copies, waits for them, and re-layouts  0.51 us (1%)
    pallas_call x1, Pallas kernels, shards(): pl.pallas_call(kernel, out_shape=pltpu.VMEM((1, BINS), f32), in_specs=[pl...  38.9 us

profile of v4, /device:TPU:1, one launch (start us, length us, event | category | flops | bytes accessed | tf_op | source)
XLA Modules:
  0.0 39.5 jit_solution(12667701561370349351)
XLA Ops:
  0.0 38.9 %radiometer.1 = f32[1,128]{1,0:T(1,128)S(1)} custom-call(bf16[128,128]{1,0:T(8,128)(2,1)} %bitcast.12, s32[2]{0:T(128)} %valid_hbm.1, f32[384,128]{1,0:T(8,128)} %bitcast.10, f32[384,128]{1,0:T(8,128)} %bitcast.11, s32[16,128]{1,0:T(8,128)} %bitcast.13), custom_call_target="tpu_custom_call" | custom-call | tf_op jit(solution)/shard_map/radiometer/pallas_call | solution.py:372
  39.0 0.5 %slice_bitcast_fusion = f32[96]{0:T(128)} fusion(f32[1,128]{1,0:T(1,128)S(1)} %radiometer.1), kind=kLoop, calls=%fused_computation | loop fusion | bytes 768 | tf_op jit(solution)/shard_map/slice | solution.py:412

commit v5 on v3

--- a/solution.py
+++ b/solution.py
@@ -121,6 +121,19 @@
     ]
     for load in loads:
         load.start()
+    pl.semaphore_wait(barrier, 7 + 7 + 3 + 2)
+
+    @pl.loop(1, 4)
+    def _(r):
+        tell(plane_sem, x_peer(r))
+
+    tell(plane_sem, core_peer)
+
+    hl = pltpu.make_async_remote_copy(
+        src_ref=spec_hbm, dst_ref=other_v, send_sem=hl_send, recv_sem=hl_recv,
+        device_id=((det + 2) % N_DET, tm), device_id_type=MESH,
+    )
+    hl.start()
     loads[0].wait()
 
     own = own_v[...].astype(jnp.float32)
@@ -131,6 +144,23 @@
     sums = jnp.where(row8 == 0, seg0, jnp.where(row8 == 1, seg1, 0.0))
     squares[...] = sums
     squares_all[det] = sums
+
+    sq_copies = [
+        pltpu.make_async_remote_copy(
+            src_ref=squares, dst_ref=squares_all.at[det],
+            send_sem=sq_send.at[r - 1], recv_sem=sq_recv.at[r - 1],
+            device_id=((det + r) % N_DET, tm), device_id_type=MESH,
+        )
+        for r in range(1, N_DET)
+    ]
+    for copy in sq_copies:
+        copy.start()
+
+    pl.semaphore_wait(plane_sem, 4)
+
+    for distance in (1, 3, -2):
+        d, chip_y = chip_at(distance)
+        tell(space_sem, (d, z * N_XY + x * 4 + chip_y))
 
     for load in loads[1:]:
         load.wait()
@@ -153,36 +183,6 @@
     pick_real = jnp.where(is_imag == 0, chosen, 0.0).astype(jnp.bfloat16)
     pick_imag = jnp.where(is_imag == 1, chosen, 0.0).astype(jnp.bfloat16)
     pick = jnp.concatenate([pick_real, pick_imag], axis=1)
-
-    pl.semaphore_wait(barrier, 7 + 7 + 3 + 2)
-
-    @pl.loop(1, 4)
-    def _(r):
-        tell(plane_sem, x_peer(r))
-
-    tell(plane_sem, core_peer)
-
-    hl = pltpu.make_async_remote_copy(
-        src_ref=own_v, dst_ref=other_v, send_sem=hl_send, recv_sem=hl_recv,
-        device_id=((det + 2) % N_DET, tm), device_id_type=MESH,
-    )
-    hl.start()
-    sq_copies = [
-        pltpu.make_async_remote_copy(
-            src_ref=squares, dst_ref=squares_all.at[det],
-            send_sem=sq_send.at[r - 1], recv_sem=sq_recv.at[r - 1],
-            device_id=((det + r) % N_DET, tm), device_id_type=MESH,
-        )
-        for r in range(1, N_DET)
-    ]
-    for copy in sq_copies:
-        copy.start()
-
-    pl.semaphore_wait(plane_sem, 4)
-
-    for distance in (1, 3, -2):
-        d, chip_y = chip_at(distance)
-        tell(space_sem, (d, z * N_XY + x * 4 + chip_y))
 
     hl.wait_recv()
     other = other_v[...].astype(jnp.float32)

time: 39.8 us -> 39.6 us (level)
  no operation moved by 1% of the time
where the time goes in v5:
time: 39.6 us; the launch traced here: 39.5 us
  Pallas kernels  39 us (98%)
  local copies, waits for them, and re-layouts  0.51 us (1%)
    pallas_call x1, Pallas kernels, shards(): pl.pallas_call(kernel, out_shape=pltpu.VMEM((1, BINS), f32), in_specs=[pl...  39 us

profile of v5, /device:TPU:1, one launch (start us, length us, event | category | flops | bytes accessed | tf_op | source)
XLA Modules:
  0.0 39.5 jit_solution(9836810709519000697)
XLA Ops:
  0.0 39.0 %radiometer.1 = f32[1,128]{1,0:T(1,128)S(1)} custom-call(bf16[128,128]{1,0:T(8,128)(2,1)} %bitcast.12, s32[2]{0:T(128)} %valid_hbm.1, f32[384,128]{1,0:T(8,128)} %bitcast.10, f32[384,128]{1,0:T(8,128)} %bitcast.11, s32[16,128]{1,0:T(8,128)} %bitcast.13), custom_call_target="tpu_custom_call" | custom-call | tf_op jit(solution)/shard_map/radiometer/pallas_call | solution.py:371
  39.0 0.5 %slice_bitcast_fusion = f32[96]{0:T(128)} fusion(f32[1,128]{1,0:T(1,128)S(1)} %radiometer.1), kind=kLoop, calls=%fused_computation | loop fusion | bytes 768 | tf_op jit(solution)/shard_map/slice | solution.py:411

commit v6 on v4

--- a/solution.py
+++ b/solution.py
@@ -167,7 +167,6 @@
         src_ref=own_v, dst_ref=other_v, send_sem=hl_send, recv_sem=hl_recv,
         device_id=(rem(det + 2, N_DET), tm), device_id_type=MESH,
     )
-    hl.start()
     sq_copies = [
         pltpu.make_async_remote_copy(
             src_ref=squares, dst_ref=squares_all.at[det],
@@ -178,6 +177,7 @@
     ]
     for copy in sq_copies:
         copy.start()
+    hl.start()
 
     pl.semaphore_wait(plane_sem, 4)
 
@@ -185,13 +185,6 @@
         d, chip_y = chip_at(distance)
         tell(space_sem, (d, z * N_XY + x * 4 + chip_y))
 
-    hl.wait_recv()
-    other = other_v[...].astype(jnp.float32)
-    own_up = pltpu.roll(own, BINS - 1, 0)
-    other_up = pltpu.roll(other, BINS - 1, 0)
-    sign = (1 - 2 * k).astype(jnp.float32)
-    cross_real = own * other + own_up * other_up
-    cross_imag = (own * other_up - own_up * other) * sign
     for copy in sq_copies:
         copy.wait_recv()
     total = lambda a: jnp.sum(a, axis=1, keepdims=True) / 8192.0 + 1e-06
@@ -200,6 +193,14 @@
     flags = jnp.where(iota((8, 1), 0) == 0, valid_s[0], valid_s[1]).astype(jnp.float32)
     weight = flags / (power_h * power_l)
     weights = jnp.where(iota((BINS, 1), 0) < 64, weight[0:1], weight[1:2])
+
+    hl.wait_recv()
+    other = other_v[...].astype(jnp.float32)
+    own_up = pltpu.roll(own, BINS - 1, 0)
+    other_up = pltpu.roll(other, BINS - 1, 0)
+    sign = (1 - 2 * k).astype(jnp.float32)
+    cross_real = own * other + own_up * other_up
+    cross_imag = (own * other_up - own_up * other) * sign
     cross = jnp.concatenate([cross_real * weights, cross_imag * weights], axis=0)
     rows = jnp.dot(pick, cross.astype(jnp.bfloat16), preferred_element_type=jnp.float32)
     send2.reshape(4 * N_TM, BINS)[...] = rows.astype(jnp.bfloat16)
@@ -292,21 +293,24 @@
         [jnp.dot(p, got, preferred_element_type=jnp.float32) for p in perms], axis=1
     ).astype(jnp.bfloat16)
 
+    def stage3(r, tile):
+        return pltpu.make_async_remote_copy(
+            src_ref=part.at[tile], dst_ref=parts.at[zh, tile],
+            send_sem=s3_send, recv_sem=s3_recv,
+            device_id=zh_peer(r), device_id_type=MESH,
+        )
+
+    def send_tile(tile):
+        @pl.loop(1, N_ZH)
+        def _(r):
+            stage3(r, tile).start()
+
     for ch in range(CHUNKS):
         product = jnp.dot(slab, kmat[ch], preferred_element_type=jnp.float32)
         turned = rot_cos[ch] * product[:, :BINS] - rot_sin[ch] * product[:, BINS:]
-        part[ch : ch + 1, :] = jnp.sum(turned, axis=0, keepdims=True)
-
-    def stage3(r):
-        return pltpu.make_async_remote_copy(
-            src_ref=part, dst_ref=parts.at[zh],
-            send_sem=s3_send, recv_sem=s3_recv,
-            device_id=zh_peer(r), device_id_type=MESH,
-        )
-
-    @pl.loop(1, N_ZH)
-    def _(r):
-        stage3(r).start()
+        part[ch // 4, ch % 4 : ch % 4 + 1, :] = jnp.sum(turned, axis=0, keepdims=True)
+        if ch % 4 == 3:
+            send_tile(ch // 4)
 
     parts[zh] = part[...]
     pltpu.make_async_copy(
@@ -315,7 +319,7 @@
 
     sums = [jnp.zeros((8, BINS), jnp.float32) for _ in range(TILES_SUM)]
     for p in range(N_ZH):
-        terms = parts[p]
+        terms = parts.reshape(N_ZH * 8, BINS)[8 * p : 8 * p + 8, :]
         for j in range(TILES_SUM):
             sums[j] += terms * masks[p, j]
     for j in range(TILES_SUM):
@@ -390,8 +394,8 @@
             pltpu.VMEM((CHUNKS, 256, BINS), f32),
             pltpu.VMEM((CHUNKS, 256, BINS), f32),
             pltpu.VMEM((N_ZH, TILES_SUM, 8, BINS), f32),
-            pltpu.VMEM((8, BINS), f32),
-            pltpu.VMEM((N_ZH, 8, BINS), f32),
+            pltpu.VMEM((2, 4, BINS), f32),
+            pltpu.VMEM((N_ZH, 2, 4, BINS), f32),
             pltpu.VMEM((32, BINS), f32),
             pltpu.VMEM((N_XYK, 1, BINS), f32),
             pltpu.VMEM((N_XYK, 1, BINS), f32),

time: 39.6 us -> 39.7 us (level)
  no operation moved by 1% of the time
where the time goes in v6:
time: 39.7 us; the launch traced here: 39.6 us
  Pallas kernels  39.1 us (98%)
  local copies, waits for them, and re-layouts  0.51 us (1%)
    pallas_call x1, Pallas kernels, shards(): pl.pallas_call(kernel, out_shape=pltpu.VMEM((1, BINS), f32), in_specs=[pl...  39.1 us

profile of v6, /device:TPU:1, one launch (start us, length us, event | category | flops | bytes accessed | tf_op | source)
XLA Modules:
  0.0 39.6 jit_solution(13337747592932693293)
XLA Ops:
  0.0 39.1 %radiometer.1 = f32[1,128]{1,0:T(1,128)S(1)} custom-call(bf16[128,128]{1,0:T(8,128)(2,1)} %bitcast.12, s32[2]{0:T(128)} %valid_hbm.1, f32[384,128]{1,0:T(8,128)} %bitcast.10, f32[384,128]{1,0:T(8,128)} %bitcast.11, s32[16,128]{1,0:T(8,128)} %bitcast.13), custom_call_target="tpu_custom_call" | custom-call | tf_op jit(solution)/shard_map/radiometer/pallas_call | solution.py:376
  39.1 0.5 %slice_bitcast_fusion = f32[96]{0:T(128)} fusion(f32[1,128]{1,0:T(1,128)S(1)} %radiometer.1), kind=kLoop, calls=%fused_computation | loop fusion | bytes 768 | tf_op jit(solution)/shard_map/slice | solution.py:416
